TPU v7x, 32 devices: a whole 2x2x4 slice. The times are simulated.
32 devices in a mesh: dp: 32 (over z, y, x, core).
Axes of the slice: x: 2, y: 2, z: 4, core: 2. Of those that a mesh axis runs over, the one named last changes fastest.
Arguments:
- patches: bfloat16 [2, 64, 2, 225, 768], P(None, 'dp'), may hold values from -6 to 6
- visible: int32 [2, 64, 128], P(None, 'dp'), may hold values from 0 to 224, as said below
- valid_mask: int32 [2, 64, 128], P(None, 'dp'), may hold values from 0 to 1, as said below
- norm1_gain: float32 [2, 768], replicated, may hold values from 0.25 to 1.75
- norm1_shift: float32 [2, 768], replicated, may hold values from -1.75 to 1.75
- qkv_weight: bfloat16 [2, 768, 2304], replicated, may hold values from -0.21875 to 0.21875
- out_weight: bfloat16 [2, 768, 768], replicated, may hold values from -1.75 to 1.75
- norm2_gain: float32 [2, 768], replicated, may hold values from 0.25 to 1.75
- norm2_shift: float32 [2, 768], replicated, may hold values from -1.75 to 1.75
- up_weight: bfloat16 [2, 768, 3072], replicated, may hold values from -0.21875 to 0.21875
- up_bias: float32 [2, 3072], replicated, may hold values from -1.75 to 1.75
- down_weight: bfloat16 [2, 3072, 768], replicated, may hold values from -0.109375 to 0.109375
Outputs:
- contrast_loss: float32 [], replicated
- patches_grad: float32 [2, 64, 2, 225, 768], P(None, 'dp')
- grad_norm1_gain: float32 [1536], P('dp')
- grad_norm1_shift: float32 [1536], P('dp')
- grad_qkv_weight: float32 [1536, 2304], P('dp')
- grad_out_weight: float32 [1536, 768], P('dp')
- grad_norm2_gain: float32 [1536], P('dp')
- grad_norm2_shift: float32 [1536], P('dp')
- grad_up_weight: float32 [1536, 3072], P('dp')
- grad_up_bias: float32 [6144], P('dp')
- grad_down_weight: float32 [6144, 768], P('dp')
Inputs may be any that keep to these rules, and one draw needn't show every extreme that they name: `visible`: the 128 entries of an image are distinct patch numbers of its 15 x 15 grid, row-major. `valid_mask`: in each image the ones come first; each image has 32 to 128 ones, and every micro-batch has an image with exactly 32 and one with exactly 128.
All inputs are finite; a program needn't handle non-finite values.
Results may differ from a plain program's by a relative error of at most 0.0082.
Values sent between devices are 32-bit elements; how exact they have to be, the bound alone decides.
A program may use at most 256 MiB of HBM per device.

v0:
```python
import math

import jax
import jax.numpy as jnp
from jax import lax
from jax.sharding import PartitionSpec as P

HEADS = 12
HEAD_DIM = 64
GRID = 15


norm_epsilon = 1e-06
unit_epsilon = 1e-06
logit_scale = 100.0
masked_score = -1e30
highest = lax.Precision.HIGHEST


def exact_gelu(values_in):
    return jax.nn.gelu(values_in, approximate=False)


def layer_norm(values_in, gain_vec, shift_vec):
    centre = values_in - jnp.mean(values_in, axis=-1, keepdims=True)
    inverse = lax.rsqrt(jnp.mean(centre * centre, axis=-1, keepdims=True) + norm_epsilon)
    normed = centre * inverse
    return (normed * gain_vec + shift_vec, normed, inverse)


def norm_back(grad_out, normed, inverse, gain_vec):
    grad_normed = grad_out * gain_vec
    mean_plain = jnp.mean(grad_normed, axis=-1, keepdims=True)
    mean_normed = jnp.mean(grad_normed * normed, axis=-1, keepdims=True)
    grad_in = inverse * (grad_normed - mean_plain - normed * mean_normed)
    return (grad_in, jnp.sum(grad_out * normed, axis=0), jnp.sum(grad_out, axis=0))


def alibi_bias(visible_rows):
    rows_pos = (visible_rows // GRID).astype(jnp.float32)
    cols_pos = (visible_rows % GRID).astype(jnp.float32)
    rows_gap = rows_pos[:, :, None] - rows_pos[:, None, :]
    cols_gap = cols_pos[:, :, None] - cols_pos[:, None, :]
    distance = jnp.sqrt(rows_gap * rows_gap + cols_gap * cols_gap)
    slopes = jnp.exp2(-8.0 * (jnp.arange(HEADS, dtype=jnp.float32) + 1.0) / HEADS)
    return -slopes[None, :, None, None] * distance[:, None, :, :]


def split_heads(packed):
    images, slot_count, _ = packed.shape
    shaped = packed.reshape(images, slot_count, 3, HEADS, HEAD_DIM)
    return (shaped[:, :, 0], shaped[:, :, 1], shaped[:, :, 2])


def attention_scores(queries, key_rows, score_bias, key_ok):
    scores = jnp.einsum("iqhd,ikhd->ihqk", queries, key_rows, preferred_element_type=jnp.float32)
    scores = scores * (1.0 / math.sqrt(HEAD_DIM)) + score_bias
    return jnp.where(key_ok, scores, masked_score)


def encode_forward(tokens_in, visible_rows, mask_rows, params):
    gain_one, shift_one, w_qkv, w_out, gain_two, shift_two, w_up, b_up, w_down = params
    images, slot_count, model_width = tokens_in.shape
    flat_in = tokens_in.reshape(images * slot_count, model_width)
    hidden_one, normed_one, inverse_one = layer_norm(flat_in, gain_one, shift_one)
    hidden_one = hidden_one.astype(jnp.bfloat16)
    packed = jnp.dot(hidden_one, w_qkv, preferred_element_type=jnp.float32).astype(jnp.bfloat16)
    packed = packed.reshape(images, slot_count, 3 * model_width)
    queries, key_rows, value_rows = split_heads(packed)
    score_bias = alibi_bias(visible_rows)
    key_ok = (mask_rows > 0)[:, None, None, :]
    scores = attention_scores(queries, key_rows, score_bias, key_ok)
    row_max = jnp.max(scores, axis=-1, keepdims=True)
    exponent = jnp.exp(scores - row_max)
    row_total = jnp.sum(exponent, axis=-1, keepdims=True)
    attention = exponent / row_total
    log_total = row_max + jnp.log(row_total)
    attended = jnp.einsum(
        "ihqk,ikhd->iqhd",
        attention.astype(jnp.bfloat16),
        value_rows,
        preferred_element_type=jnp.float32,
    )
    attended = attended.reshape(images * slot_count, model_width).astype(jnp.bfloat16)
    mixed_rows = flat_in + jnp.dot(attended, w_out, preferred_element_type=jnp.float32)
    hidden_two, normed_two, inverse_two = layer_norm(mixed_rows, gain_two, shift_two)
    hidden_two = hidden_two.astype(jnp.bfloat16)
    upper_pre = jnp.dot(hidden_two, w_up, preferred_element_type=jnp.float32) + b_up
    active, gelu_back = jax.vjp(exact_gelu, upper_pre)
    active = active.astype(jnp.bfloat16)
    output_rows = mixed_rows + jnp.dot(active, w_down, preferred_element_type=jnp.float32)
    weight_mask = mask_rows.astype(jnp.float32)
    counted = jnp.sum(weight_mask, axis=1)[:, None]
    pooled = (
        jnp.sum(
            output_rows.reshape(images, slot_count, model_width) * weight_mask[:, :, None], axis=1
        )
        / counted
    )
    inverse_unit = lax.rsqrt(jnp.sum(pooled * pooled, axis=-1, keepdims=True) + unit_epsilon)
    unit_rows = pooled * inverse_unit
    saved = (
        normed_one,
        inverse_one,
        hidden_one,
        packed,
        score_bias,
        key_ok,
        log_total,
        attended,
        normed_two,
        inverse_two,
        hidden_two,
        gelu_back,
        active,
        weight_mask,
        counted,
        unit_rows,
        inverse_unit,
    )
    return (unit_rows, saved)


def encode_backward(grad_unit, saved, params):
    (
        normed_one,
        inverse_one,
        hidden_one,
        packed,
        score_bias,
        key_ok,
        log_total,
        attended,
        normed_two,
        inverse_two,
        hidden_two,
        gelu_back,
        active,
        weight_mask,
        counted,
        unit_rows,
        inverse_unit,
    ) = saved
    gain_one, shift_one, w_qkv, w_out, gain_two, shift_two, w_up, b_up, w_down = params
    images, slot_count, three_width = packed.shape
    model_width = three_width // 3
    head_scale = 1.0 / math.sqrt(HEAD_DIM)
    grad_pooled = inverse_unit * (
        grad_unit - unit_rows * jnp.sum(unit_rows * grad_unit, axis=-1, keepdims=True)
    )
    grad_output = weight_mask[:, :, None] * (grad_pooled / counted)[:, None, :]
    grad_output = grad_output.reshape(images * slot_count, model_width)
    grad_output_low = grad_output.astype(jnp.bfloat16)
    grad_down = jnp.dot(active.T, grad_output_low, preferred_element_type=jnp.float32)
    grad_active = jnp.dot(grad_output_low, w_down.T, preferred_element_type=jnp.float32)
    grad_upper = gelu_back(grad_active)[0].astype(jnp.bfloat16)
    grad_up = jnp.dot(hidden_two.T, grad_upper, preferred_element_type=jnp.float32)
    grad_bias = jnp.sum(grad_upper.astype(jnp.float32), axis=0)
    grad_hidden_two = jnp.dot(grad_upper, w_up.T, preferred_element_type=jnp.float32)
    grad_norm_two, grad_gain_two, grad_shift_two = norm_back(
        grad_hidden_two, normed_two, inverse_two, gain_two
    )
    grad_mixed = grad_output + grad_norm_two
    grad_mixed_low = grad_mixed.astype(jnp.bfloat16)
    grad_out = jnp.dot(attended.T, grad_mixed_low, preferred_element_type=jnp.float32)
    grad_attended = jnp.dot(grad_mixed_low, w_out.T, preferred_element_type=jnp.float32).astype(
        jnp.bfloat16
    )
    grad_attended = grad_attended.reshape(images, slot_count, HEADS, HEAD_DIM)
    queries, key_rows, value_rows = split_heads(packed)
    scores = attention_scores(queries, key_rows, score_bias, key_ok)
    attention = jnp.exp(scores - log_total)
    grad_value = jnp.einsum(
        "ihqk,iqhd->ikhd",
        attention.astype(jnp.bfloat16),
        grad_attended,
        preferred_element_type=jnp.float32,
    )
    grad_attention = jnp.einsum(
        "iqhd,ikhd->ihqk", grad_attended, value_rows, preferred_element_type=jnp.float32
    )
    grad_scores = attention * (
        grad_attention - jnp.sum(attention * grad_attention, axis=-1, keepdims=True)
    )
    grad_scores = grad_scores.astype(jnp.bfloat16)
    grad_query = (
        jnp.einsum("ihqk,ikhd->iqhd", grad_scores, key_rows, preferred_element_type=jnp.float32)
        * head_scale
    )
    grad_key = (
        jnp.einsum("ihqk,iqhd->ikhd", grad_scores, queries, preferred_element_type=jnp.float32)
        * head_scale
    )
    grad_packed = jnp.stack([grad_query, grad_key, grad_value], axis=2).astype(jnp.bfloat16)
    grad_packed = grad_packed.reshape(images * slot_count, three_width)
    grad_qkv = jnp.dot(hidden_one.T, grad_packed, preferred_element_type=jnp.float32)
    grad_hidden_one = jnp.dot(grad_packed, w_qkv.T, preferred_element_type=jnp.float32)
    grad_norm_one, grad_gain_one, grad_shift_one = norm_back(
        grad_hidden_one, normed_one, inverse_one, gain_one
    )
    grad_tokens = (grad_mixed + grad_norm_one).reshape(images, slot_count, model_width)
    return (
        grad_tokens,
        (
            grad_gain_one,
            grad_shift_one,
            grad_qkv,
            grad_out,
            grad_gain_two,
            grad_shift_two,
            grad_up,
            grad_bias,
            grad_down,
        ),
    )


def join_pair(optical_part, radar_part):
    joined = jnp.stack([optical_part, radar_part])
    return joined.reshape((2 * optical_part.shape[0],) + optical_part.shape[1:])


def on_device(
    patches,
    visible,
    valid_mask,
    norm1_gain,
    norm1_shift,
    qkv_weight,
    out_weight,
    norm2_gain,
    norm2_shift,
    up_weight,
    up_bias,
    down_weight,
):
    micro_count, images, _, patch_count, model_width = patches.shape
    scale_loss = 1.0 / (2 * images * lax.axis_size("dp") * micro_count)
    image_start = lax.axis_index("dp") * images
    image_index = jnp.arange(images)[:, None]
    accum = [None, None]
    grad_cells = []
    loss_sum = jnp.zeros((), jnp.float32)
    for micro_index in range(micro_count):
        unit_list = []
        saved_list = []
        param_list = []
        for modality in range(2):
            params = (
                norm1_gain[modality],
                norm1_shift[modality],
                qkv_weight[modality],
                out_weight[modality],
                norm2_gain[modality],
                norm2_shift[modality],
                up_weight[modality],
                up_bias[modality],
                down_weight[modality],
            )
            tokens_in = jnp.take_along_axis(
                patches[micro_index, :, modality], visible[micro_index][:, :, None], axis=1
            )
            unit_rows, saved = encode_forward(
                tokens_in.astype(jnp.float32), visible[micro_index], valid_mask[micro_index], params
            )
            unit_list.append(unit_rows)
            saved_list.append(saved)
            param_list.append(params)
        all_optical, all_radar = (
            lax.all_gather(unit_list[0], "dp", axis=0, tiled=True),
            lax.all_gather(unit_list[1], "dp", axis=0, tiled=True),
        )
        batch_size = all_optical.shape[0]
        logits = logit_scale * jnp.dot(all_optical, all_radar.T, precision=highest)
        identity = (jnp.arange(batch_size)[:, None] == jnp.arange(batch_size)[None, :]).astype(
            jnp.float32
        )
        diagonal = jnp.sum(logits * identity, axis=1)
        loss_sum = (
            loss_sum
            + jnp.sum(jax.nn.logsumexp(logits, axis=1) - diagonal)
            + jnp.sum(jax.nn.logsumexp(logits, axis=0) - diagonal)
        )
        labels = image_start + jnp.arange(images)
        onehot = (jnp.arange(batch_size)[None, :] == labels[:, None]).astype(jnp.float32)
        logits_optical = logit_scale * jnp.dot(unit_list[0], all_radar.T, precision=highest)
        logits_radar = logit_scale * jnp.dot(unit_list[1], all_optical.T, precision=highest)
        grad_lo = scale_loss * (jax.nn.softmax(logits_optical, axis=1) - onehot)
        grad_lr = scale_loss * (jax.nn.softmax(logits_radar, axis=1) - onehot)
        grad_optical = logit_scale * jnp.dot(grad_lo, all_radar, precision=highest)
        grad_radar = logit_scale * jnp.dot(grad_lr, all_optical, precision=highest)
        spread_optical = logit_scale * jnp.dot(grad_lr.T, unit_list[1], precision=highest)
        spread_radar = logit_scale * jnp.dot(grad_lo.T, unit_list[0], precision=highest)
        back_optical, back_radar = (
            lax.psum_scatter(spread_optical, "dp", scatter_dimension=0, tiled=True),
            lax.psum_scatter(spread_radar, "dp", scatter_dimension=0, tiled=True),
        )
        grad_optical = grad_optical + back_optical
        grad_radar = grad_radar + back_radar
        grad_units = (grad_optical, grad_radar)
        cells_now = []
        for modality in range(2):
            grad_tokens, grad_terms = encode_backward(
                grad_units[modality], saved_list[modality], param_list[modality]
            )
            if accum[modality] is None:
                accum[modality] = grad_terms
            else:
                accum[modality] = jax.tree.map(jnp.add, accum[modality], grad_terms)
            cell_grad = jnp.zeros((images, patch_count, model_width), jnp.float32)
            cells_now.append(cell_grad.at[image_index, visible[micro_index]].add(grad_tokens))
        grad_cells.append(jnp.stack(cells_now, axis=1))
    joined = jax.tree.map(join_pair, accum[0], accum[1])
    shards = (
        lax.psum_scatter(joined[0], "dp", scatter_dimension=0, tiled=True),
        lax.psum_scatter(joined[1], "dp", scatter_dimension=0, tiled=True),
        lax.psum_scatter(joined[2], "dp", scatter_dimension=0, tiled=True),
        lax.psum_scatter(joined[3], "dp", scatter_dimension=0, tiled=True),
        lax.psum_scatter(joined[4], "dp", scatter_dimension=0, tiled=True),
        lax.psum_scatter(joined[5], "dp", scatter_dimension=0, tiled=True),
        lax.psum_scatter(joined[6], "dp", scatter_dimension=0, tiled=True),
        lax.psum_scatter(joined[7], "dp", scatter_dimension=0, tiled=True),
        lax.psum_scatter(joined[8], "dp", scatter_dimension=0, tiled=True),
    )
    contrast_loss = loss_sum * scale_loss
    patches_grad = jnp.stack(grad_cells, axis=0)
    return (
        contrast_loss,
        patches_grad,
        shards[0],
        shards[1],
        shards[2],
        shards[3],
        shards[4],
        shards[5],
        shards[6],
        shards[7],
        shards[8],
    )


def solution(mesh):
    in_specs = (
        P(None, "dp", None, None, None),
        P(None, "dp", None),
        P(None, "dp", None),
        P(),
        P(),
        P(),
        P(),
        P(),
        P(),
        P(),
        P(),
        P(),
    )
    out_specs = (
        P(),
        P(None, "dp", None, None, None),
        P("dp"),
        P("dp"),
        P("dp", None),
        P("dp", None),
        P("dp"),
        P("dp"),
        P("dp", None),
        P("dp"),
        P("dp", None),
    )
    return jax.shard_map(
        on_device, mesh=mesh, in_specs=in_specs, out_specs=out_specs, check_vma=False
    )
```

profile of v0, /device:TPU:0, one launch (start us, length us, event | category | flops | bytes accessed | tf_op | source)
XLA Modules:
  0.0 1262.0 jit_solution(18105332294909847470)
XLA Ops:
  14.4 7.4 fusion.310
  46.9 4.4 convolution_convert_fusion.3
  65.6 3.5 reshape_reshape.17
  75.9 12.3 multiply_convert_fusion.3
  89.6 9.9 multiply_convert_fusion.2
  101.9 43.7 %all-gather = f32[32,2,768]{2,1,0:T(2,128)S(1)} all-gather(f32[1,2,768]{2,1,0:T(2,128)S(1)} %fusion.298), channel_id=1, replica_groups=mesh['dp'=32] {'dp'}, dimensions={0}, use_global_device_ids=true | all-gather | bytes 202752 | tf_op jit(solution)/shard_map/all_gather | solution.py:270
  147.0 37.1 %all-gather.1 = f32[32,2,768]{2,1,0:T(2,128)S(1)} all-gather(f32[1,2,768]{2,1,0:T(2,128)S(1)} %fusion.299), channel_id=1, replica_groups=mesh['dp'=32] {'dp'}, dimensions={0}, use_global_device_ids=true | all-gather | bytes 202752 | tf_op jit(solution)/shard_map/all_gather | solution.py:271
  185.0 4.1 convolution_convert_fusion.1
  189.1 2.6 copy.136
  191.8 2.8 reshape_reshape.18
  200.4 12.2 multiply_convert_fusion.1
  217.5 3.2 reshape_reshape.19
  226.2 11.6 multiply_convert_fusion
  241.2 41.1 %all-gather.2 = f32[32,2,768]{2,1,0:T(2,128)} all-gather(f32[1,2,768]{2,1,0:T(2,128)S(1)} %fusion.300), channel_id=1, replica_groups=mesh['dp'=32] {'dp'}, dimensions={0}, use_global_device_ids=true | all-gather | bytes 202752 | tf_op jit(solution)/shard_map/all_gather | solution.py:270
  286.1 39.8 %all-gather.3 = f32[32,2,768]{2,1,0:T(2,128)} all-gather(f32[1,2,768]{2,1,0:T(2,128)S(1)} %fusion.301), channel_id=1, replica_groups=mesh['dp'=32] {'dp'}, dimensions={0}, use_global_device_ids=true | all-gather | bytes 202752 | tf_op jit(solution)/shard_map/all_gather | solution.py:271
  350.6 121.9 %all-reduce.13.cloned.1.call-done = (f32[64,768]{1,0:T(8,128)}, f32[64,768]{1,0:T(8,128)}, f32[64,768]{1,0:T(8,128)}, f32[64,768]{1,0:T(8,128)}) async-done(((f32[64,768]{1,0:T(8,128)}, f32[64,768]{1,0:T(8,128)}, f32[64,768]{1,0:T(8,128)}, f32[64,768]{1,0:T(8,128)}), (f32[64,768]{1,0:T(8,128)}, f32[64,768]{1,0:T(8,128)}, f32[64,768]{1,0:T(8,128)}, f32[64,768]{1,0:T(8,128)})) %all-reduce.13.cloned.1.call-update) | async-done | bytes 786448
  481.5 7.0 convert_reduce_fusion.3
  488.6 5.2 multiply_reduce_fusion.7
  493.9 4.6 convert_reduce_fusion.2
  498.7 3.4 fusion.200
  508.0 3.0 fusion.152
  516.0 5.3 convert_reduce_fusion.1
  521.3 5.2 multiply_reduce_fusion.5
  526.7 4.8 convert_reduce_fusion
  531.5 3.4 fusion.198
  580.8 4.0 add_bitcast_fusion.4
  584.8 4.1 add_bitcast_fusion.5
  588.9 11.2 pad_maximum_fusion.2
  601.2 3.6 fusion.303
  606.5 3.2 add_bitcast_fusion.2
  611.4 6.8 pad_maximum_fusion
  625.7 7.3 pad_maximum_fusion.1
  639.2 3.3 fusion.52
  643.4 3.9 multiply_reduce_fusion.9
  647.4 3.2 fusion.50
  654.7 24.1 %scatter_fusion.3 = f32[2,225,768]{2,0,1:T(2,128)S(1)} fusion(f32[2,225,768]{2,0,1:T(2,128)S(1)} %broadcast.955.clone, s32[256]{0:T(256)S(1)} %copy-done.1, f32[256,768]{1,0:T(8,128)} %get-tuple-element.187), kind=kCustom, calls=%fused_computation.7 | custom fusion | flops 196608 | bytes 2361344 | tf_op jit(solution)/shard_map/scatter-add | solution.py:311
  678.9 4.0 multiply_add_fusion.7
  683.3 24.1 %scatter_fusion.2 = f32[2,225,768]{2,0,1:T(2,128)S(1)} fusion(f32[2,225,768]{2,0,1:T(2,128)S(1)} %broadcast.955.clone.1, s32[256]{0:T(256)S(1)} %copy-done.1, f32[256,768]{1,0:T(8,128)} %get-tuple-element.185), kind=kCustom, calls=%fused_computation.6 | custom fusion | flops 196608 | bytes 2361344 | tf_op jit(solution)/shard_map/scatter-add | solution.py:311
  707.8 24.1 %scatter_fusion.1 = f32[2,225,768]{2,0,1:T(2,128)S(1)} fusion(f32[2,225,768]{2,0,1:T(2,128)S(1)} %broadcast.955.clone.2, s32[256]{0:T(256)S(1)} %copy-done, f32[256,768]{1,0:T(8,128)} %get-tuple-element.186), kind=kCustom, calls=%fused_computation.5 | custom fusion | flops 196608 | bytes 2361344 | tf_op jit(solution)/shard_map/scatter-add | solution.py:311
  733.3 24.2 %scatter_fusion = f32[2,225,768]{2,0,1:T(2,128)S(1)} fusion(f32[2,225,768]{2,0,1:T(2,128)S(1)} %broadcast.955.clone.3, s32[256]{0:T(256)S(1)} %copy-done, f32[256,768]{1,0:T(8,128)} %get-tuple-element.184), kind=kCustom, calls=%fused_computation.4 | custom fusion | flops 196608 | bytes 2361344 | tf_op jit(solution)/shard_map/scatter-add | solution.py:311
  757.6 2.8 maximum_bitcast_fusion.1
  760.4 2.8 maximum_bitcast_fusion
  763.2 4.3 pad_maximum_fusion.3
  767.6 5.3 copy.177
  773.4 41.6 %all-reduce.9 = (f32[1536]{0:T(1024)S(1)}, f32[1536]{0:T(1024)S(1)}, f32[1536]{0:T(1024)S(1)}, f32[1536]{0:T(1024)S(1)}, f32[6144]{0:T(1024)S(1)}) all-reduce(f32[1536]{0:T(1024)S(1)} %reshape.1178, f32[1536]{0:T(1024)S(1)} %reshape.1179, f32[1536]{0:T(1024)S(1)} %reshape.1182, ...), channel_id=6, replica_groups=mesh['dp'=32] {'dp'}, use_global_device_ids=true, to_apply=%region_92.94.clone | all-reduce | flops 12288 | bytes 98304
  818.0 11.2 reduce-scatter.5.cloned.1.call-done
  829.1 212.6 %reduce-scatter.9.cloned.1.call-done = f32[48,3072]{1,0:T(8,128)} async-done(((f32[1536,3072]{1,0:T(8,128)}), f32[48,3072]{1,0:T(8,128)}) %reduce-scatter.9.cloned.1.call-update) | async-done | bytes 589840 | tf_op jit(solution)/shard_map/reduce_scatter | solution.py:321
  1041.7 212.5 %reduce-scatter.11.cloned.1.call-done = f32[192,768]{1,0:T(8,128)} async-done(((f32[6144,768]{1,0:T(8,128)}), f32[192,768]{1,0:T(8,128)}) %reduce-scatter.11.cloned.1.call-update) | async-done | bytes 589840 | tf_op jit(solution)/shard_map/reduce_scatter | solution.py:323
  (813 shorter events, 196.4 us)
Async XLA Ops:
  7.2 465.4 %all-reduce.13.cloned.1.call-start = ((), (), s32[]{:S(2)}) async-start(), calls=%async_computation.8 | async-start | bytes 1572864
  7.9 36.3 %copy-start.159 = (pred[2,128]{1,0:T(4,128)(4,1)}, pred[2,128]{1,0:T(4,128)(4,1)S(1)}, u32[]{:S(2)}) copy-start(pred[2,128]{1,0:T(4,128)(4,1)S(1)} %get-tuple-element.202) | copy-start | bytes 772
  7.9 36.3 %copy-start.161 = (pred[2,128]{1,0:T(4,128)(4,1)}, pred[2,128]{1,0:T(4,128)(4,1)S(1)}, u32[]{:S(2)}) copy-start(pred[2,128]{1,0:T(4,128)(4,1)S(1)} %get-tuple-element.203) | copy-start | bytes 772
  10.5 44.4 %copy-start.241 = (f32[12]{0:T(128)}, f32[12]{0:T(128)S(1)}, u32[]{:S(2)}) copy-start(f32[12]{0:T(128)S(1)} %exponential_negate_fusion) | copy-start | bytes 148
  13.0 41.9 %copy-start.234 = (pred[2,128]{1,0:T(4,128)(4,1)}, pred[2,128]{1,0:T(4,128)(4,1)S(1)}, u32[]{:S(2)}) copy-start(pred[2,128]{1,0:T(4,128)(4,1)S(1)} %get-tuple-element.197) | copy-start | bytes 772
  25.2 19.0 %copy-start.22 = (bf16[256,768]{1,0:T(8,128)(2,1)}, bf16[256,768]{1,0:T(8,128)(2,1)S(1)}, u32[]{:S(2)}) copy-start(bf16[256,768]{1,0:T(8,128)(2,1)S(1)} %gather_fusion) | copy-start | bytes 1179652
  27.2 17.0 %copy-start.26 = (bf16[256,768]{1,0:T(8,128)(2,1)}, bf16[256,768]{1,0:T(8,128)(2,1)S(1)}, u32[]{:S(2)}) copy-start(bf16[256,768]{1,0:T(8,128)(2,1)S(1)} %gather_fusion.1) | copy-start | bytes 1179652
  33.4 10.8 copy-start.28
  46.9 14.2 %copy-start.80 = (bf16[2,128,768]{2,1,0:T(8,128)(2,1)}, bf16[2,128,768]{2,1,0:T(8,128)(2,1)S(1)}, u32[]{:S(2)}) copy-start(bf16[2,128,768]{2,1,0:T(8,128)(2,1)S(1)} %get-tuple-element.167) | copy-start | bytes 1179652
  59.6 28.5 %copy-start.43 = (f32[256,768]{1,0:T(8,128)}, f32[256,768]{1,0:T(8,128)S(1)}, u32[]{:S(2)}) copy-start(f32[256,768]{1,0:T(8,128)S(1)} %get-tuple-element.248) | copy-start | bytes 2359300
  74.9 13.2 %slice-start = ((s8[9437184]{0:T(1024)(128)(4,1)}), s8[4194304]{0:T(1024)(128)(4,1)S(1)}, s32[]{:S(2)}) async-start(s8[9437184]{0:T(1024)(128)(4,1)} %bitcast.685), calls=%async_computation.9 | async-start | bytes 8388608
  74.9 14.7 %slice-start.15 = ((s8[9437184]{0:T(1024)(128)(4,1)}), s8[4194304]{0:T(1024)(128)(4,1)S(1)}, s32[]{:S(2)}) async-start(s8[9437184]{0:T(1024)(128)(4,1)} %bitcast.695), calls=%async_computation.24 | async-start | bytes 8388608
  75.5 24.1 %copy-start.19 = (f32[256,768]{1,0:T(8,128)}, f32[256,768]{1,0:T(8,128)S(1)}, u32[]{:S(2)}) copy-start(f32[256,768]{1,0:T(8,128)S(1)} %get-tuple-element.243) | copy-start | bytes 2359300
  75.5 14.0 %copy-start.175 = (f32[256]{0:T(256)}, f32[256]{0:T(256)S(1)}, u32[]{:S(2)}) copy-start(f32[256]{0:T(256)S(1)} %broadcast_multiply_fusion.22) | copy-start | bytes 3076
  75.8 13.8 %copy-start.186 = (f32[256]{0:T(256)}, f32[256]{0:T(256)S(1)}, u32[]{:S(2)}) copy-start(f32[256]{0:T(256)S(1)} %add_rsqrt_fusion.4) | copy-start | bytes 3076
  75.8 12.3 slice-start.1
  75.8 12.3 slice-start.2
  75.8 13.8 %slice-start.16 = ((s8[9437184]{0:T(1024)(128)(4,1)}), s8[4194304]{0:T(1024)(128)(4,1)S(1)}, s32[]{:S(2)}) async-start(s8[9437184]{0:T(1024)(128)(4,1)} %bitcast.695), calls=%async_computation.25 | async-start | bytes 8388608
  75.8 13.8 %slice-start.17 = ((s8[9437184]{0:T(1024)(128)(4,1)}), s8[1048576]{0:T(1024)(128)(4,1)S(1)}, s32[]{:S(2)}) async-start(s8[9437184]{0:T(1024)(128)(4,1)} %bitcast.695), calls=%async_computation.26 | async-start | bytes 2097152
  99.6 85.4 %copy-start.115 = (bf16[2,128,768]{2,1,0:T(8,128)(2,1)S(1)}, bf16[2,128,768]{2,1,0:T(8,128)(2,1)}, u32[]{:S(2)}) copy-start(bf16[2,128,768]{2,1,0:T(8,128)(2,1)} %get-tuple-element.205) | copy-start | bytes 1179652
  101.2 87.9 %copy-start.134 = (f32[2,768]{1,0:T(2,128)}, f32[2,768]{1,0:T(2,128)S(1)}, u32[]{:S(2)}) copy-start(f32[2,768]{1,0:T(2,128)S(1)} %get-tuple-element.139) | copy-start | bytes 18436
  198.9 13.7 %slice-start.3 = ((s8[9437184]{0:T(1024)(128)(4,1)}), s8[4194304]{0:T(1024)(128)(4,1)S(1)}, s32[]{:S(2)}) async-start(s8[9437184]{0:T(1024)(128)(4,1)} %bitcast.687), calls=%async_computation.12 | async-start | bytes 8388608
  198.9 16.0 %slice-start.26 = ((s8[7077888]{0:T(1024)(128)(4,1)}), s8[4194304]{0:T(1024)(128)(4,1)S(1)}, s32[]{:S(2)}) async-start(s8[7077888]{0:T(1024)(128)(4,1)} %bitcast.703), calls=%async_computation.35 | async-start | bytes 8388608
  200.1 12.5 copy-start.6
  200.1 12.5 copy-start.151
  200.3 12.2 copy-start.163
  200.4 12.2 slice-start.4
  200.4 12.2 slice-start.5
  200.4 14.5 %slice-start.27 = ((s8[7077888]{0:T(1024)(128)(4,1)}), s8[2883584]{0:T(1024)(128)(4,1)S(1)}, s32[]{:S(2)}) async-start(s8[7077888]{0:T(1024)(128)(4,1)} %bitcast.703), calls=%async_computation.36 | async-start | bytes 5767168
  225.8 11.9 copy-start.155
  226.1 11.7 slice-start.6
  226.1 11.6 copy-start.167
  226.1 11.7 slice-start.7
  226.1 11.7 slice-start.8
  226.1 11.7 copy-start.119
  226.1 11.7 copy-start.198
  330.0 12.1 copy-start.240
  345.0 473.0 %reduce-scatter.7.cloned.1.call-start = ((), (), s32[]{:S(2)}) async-start(), calls=%async_computation.5 | async-start | bytes 4866048 | tf_op jit(solution)/shard_map/reduce_scatter | solution.py:318
  481.4 12.4 slice-start.9
  481.5 12.4 slice-start.10
  516.0 10.6 slice-start.12
  516.0 10.6 slice-start.13
  553.7 275.4 %reduce-scatter.5.cloned.1.call-start = ((), (), s32[]{:S(2)}) async-start(), calls=%async_computation.4 | async-start | bytes 14598144 | tf_op jit(solution)/shard_map/reduce_scatter | solution.py:317
  600.2 441.6 %reduce-scatter.9.cloned.1.call-start = ((), (), s32[]{:S(2)}) async-start(), calls=%async_computation.6 | async-start | bytes 19464192 | tf_op jit(solution)/shard_map/reduce_scatter | solution.py:321
  618.2 636.0 %reduce-scatter.11.cloned.1.call-start = ((), (), s32[]{:S(2)}) async-start(), calls=%async_computation.7 | async-start | bytes 19464192 | tf_op jit(solution)/shard_map/reduce_scatter | solution.py:323
  639.2 11.5 slice-start.28
  654.7 24.1 %copy-start.34 = (f32[256,768]{1,0:T(8,128)S(1)}, f32[256,768]{1,0:T(8,128)}, u32[]{:S(2)}) copy-start(f32[256,768]{1,0:T(8,128)} %copy-done.32) | copy-start | bytes 2359300
  683.3 24.5 %copy-start = (s32[256]{0:T(256)S(1)}, s32[256]{0:T(256)}, u32[]{:S(2)}) copy-start(s32[256]{0:T(256)} %get-tuple-element.192) | copy-start | bytes 3076
  (234 other events, 730.8 us)
Sparse Core Ops, SparseCore 0:
  345.1 127.3 all-reduce.12
  553.8 106.0 reduce-scatter.6
  666.5 162.5 reduce-scatter.4
  836.0 205.6 reduce-scatter.8
  1048.5 205.5 reduce-scatter.10
where the time goes:
time: 1280 us; the launch traced here: 1260 us
  waiting for transfers between devices  558 us (44%)
  blocking collectives  203 us (16%)
  matrix products  196 us (15%)
  other arithmetic  183 us (14%)
  local copies, waits for them, and re-layouts  99.1 us (8%)
  between operations  21.8 us (2%)
    reduce_scatter x1, waiting for transfers between devices, on_device(): lax.psum_scatter(joined[6], 'dp', scatter_dimension=0, tiled=True)  213 us
    reduce_scatter x1, waiting for transfers between devices, on_device(): lax.psum_scatter(joined[8], 'dp', scatter_dimension=0, tiled=True)  212 us
    unnamed x6, waiting for transfers between devices  122 us
    scatter-add x4, other arithmetic, on_device(): cell_grad.at[image_index, visible[micro_index]].add(grad_tokens)  96.5 us
    all_gather x2, blocking collectives, on_device(): lax.all_gather(unit_list[0], 'dp', axis=0, tiled=True)  84.9 us
    all_gather x2, blocking collectives, on_device(): lax.all_gather(unit_list[1], 'dp', axis=0, tiled=True)  77 us
    dot_general x4, matrix products, encode_forward(): jnp.dot(hidden_two, w_up, preferred_element_type=jnp.float32) + b_up  46 us
    unnamed x1, blocking collectives  41.6 us
  transfers between devices with their start and end apart: 5, of which 4 were waited for; matrix products, arithmetic and copies ran while one was open for 17% of the time, Pallas kernels for 0%

commit v1 on v0

v1 whole, which is shorter than its diff:
```python
import functools
import math

import jax
import jax.numpy as jnp
from jax import lax
from jax.experimental import pallas as pl
from jax.experimental.pallas import tpu as pltpu
from jax.sharding import PartitionSpec as P

HEADS = 12
HEAD_DIM = 64
GRID = 15
MESH = pl.DeviceIdType.MESH

norm_epsilon = 1e-06
unit_epsilon = 1e-06
logit_scale = 100.0
masked_score = -1e30
highest = lax.Precision.HIGHEST
head_scale = 1.0 / math.sqrt(HEAD_DIM)
f32 = jnp.float32
bf16 = jnp.bfloat16


def exact_gelu(values_in):
    return jax.nn.gelu(values_in, approximate=False)


def layer_norm(values_in, gain_vec, shift_vec):
    centre = values_in - jnp.mean(values_in, axis=-1, keepdims=True)
    inverse = lax.rsqrt(jnp.mean(centre * centre, axis=-1, keepdims=True) + norm_epsilon)
    normed = centre * inverse
    return (normed * gain_vec + shift_vec, normed, inverse)


def norm_back(grad_out, normed, inverse, gain_vec):
    grad_normed = grad_out * gain_vec
    mean_plain = jnp.mean(grad_normed, axis=-1, keepdims=True)
    mean_normed = jnp.mean(grad_normed * normed, axis=-1, keepdims=True)
    grad_in = inverse * (grad_normed - mean_plain - normed * mean_normed)
    return (grad_in, jnp.sum(grad_out * normed, axis=0), jnp.sum(grad_out, axis=0))


def alibi_bias(visible_rows):
    rows_pos = (visible_rows // GRID).astype(f32)
    cols_pos = (visible_rows % GRID).astype(f32)
    rows_gap = rows_pos[:, :, None] - rows_pos[:, None, :]
    cols_gap = cols_pos[:, :, None] - cols_pos[:, None, :]
    distance = jnp.sqrt(rows_gap * rows_gap + cols_gap * cols_gap)
    slopes = jnp.exp2(-8.0 * (jnp.arange(HEADS, dtype=f32) + 1.0) / HEADS)
    return -slopes[None, :, None, None] * distance[:, None, :, :]


def split_heads(packed):
    images, slot_count, _ = packed.shape
    shaped = packed.reshape(images, slot_count, 3, HEADS, HEAD_DIM)
    return (shaped[:, :, 0], shaped[:, :, 1], shaped[:, :, 2])


def encode_forward(tokens_in, visible_rows, mask_rows, params):
    gain_one, shift_one, w_qkv, w_out, gain_two, shift_two, w_up, b_up, w_down = params
    images, slots, width = tokens_in.shape
    flat_in = tokens_in.reshape(images * slots, width)
    hidden_one, normed_one, inverse_one = layer_norm(flat_in, gain_one, shift_one)
    hidden_one = hidden_one.astype(bf16)
    packed = jnp.dot(hidden_one, w_qkv, preferred_element_type=f32).astype(bf16)
    packed = packed.reshape(images, slots, 3 * width)
    queries, keys, values = split_heads(packed)
    scores = jnp.einsum("iqhd,ikhd->ihqk", queries, keys, preferred_element_type=f32)
    scores = scores * head_scale + alibi_bias(visible_rows)
    scores = jnp.where((mask_rows > 0)[:, None, None, :], scores, masked_score)
    attention = jax.nn.softmax(scores, axis=-1)
    attended = jnp.einsum("ihqk,ikhd->iqhd", attention.astype(bf16), values, preferred_element_type=f32)
    attended = attended.reshape(images * slots, width).astype(bf16)
    mixed = flat_in + jnp.dot(attended, w_out, preferred_element_type=f32)
    hidden_two, normed_two, inverse_two = layer_norm(mixed, gain_two, shift_two)
    hidden_two = hidden_two.astype(bf16)
    upper = jnp.dot(hidden_two, w_up, preferred_element_type=f32) + b_up
    active, gelu_back = jax.vjp(exact_gelu, upper)
    active = active.astype(bf16).astype(f32)
    weight = mask_rows.astype(f32)
    active_sum = jnp.sum(active.reshape(images, slots, -1) * weight[:, :, None], axis=1)
    mixed_sum = jnp.sum(mixed.reshape(images, slots, width) * weight[:, :, None], axis=1)
    saved = (normed_one, inverse_one, hidden_one, packed, attention, attended, normed_two, inverse_two, hidden_two, gelu_back)
    return active_sum, mixed_sum, saved


def pool(active_sum, mixed_sum, mask_rows, w_down):
    counted = jnp.sum(mask_rows.astype(f32), axis=1)[:, None]
    down = jnp.dot(active_sum, w_down.astype(f32), precision=highest)
    return (mixed_sum + down) / counted


def encode_backward(grad_pooled, saved, mask_rows, params):
    normed_one, inverse_one, hidden_one, packed, attention, attended, normed_two, inverse_two, hidden_two, gelu_back = saved
    gain_one, shift_one, w_qkv, w_out, gain_two, shift_two, w_up, b_up, w_down = params
    images, slots, three_width = packed.shape
    width = three_width // 3
    rows = images * slots
    weight = mask_rows.astype(f32)
    counted = jnp.sum(weight, axis=1)[:, None]
    grad_row = grad_pooled / counted
    grad_output = (weight[:, :, None] * grad_row[:, None, :]).reshape(rows, width)
    grad_active = jnp.dot(grad_row.astype(bf16), w_down.T, preferred_element_type=f32)
    grad_active = (weight[:, :, None] * grad_active[:, None, :]).reshape(rows, -1)
    grad_upper = gelu_back(grad_active)[0].astype(bf16)
    grad_bias = jnp.sum(grad_upper.astype(f32), axis=0)
    grad_up = jnp.dot(hidden_two.T, grad_upper, preferred_element_type=f32)
    grad_hidden_two = jnp.dot(grad_upper, w_up.T, preferred_element_type=f32)
    grad_norm_two, grad_gain_two, grad_shift_two = norm_back(grad_hidden_two, normed_two, inverse_two, gain_two)
    grad_mixed = grad_output + grad_norm_two
    grad_mixed_low = grad_mixed.astype(bf16)
    grad_out = jnp.dot(attended.T, grad_mixed_low, preferred_element_type=f32)
    grad_attended = jnp.dot(grad_mixed_low, w_out.T, preferred_element_type=f32).astype(bf16)
    grad_attended = grad_attended.reshape(images, slots, HEADS, HEAD_DIM)
    queries, keys, values = split_heads(packed)
    grad_value = jnp.einsum("ihqk,iqhd->ikhd", attention.astype(bf16), grad_attended, preferred_element_type=f32)
    grad_attention = jnp.einsum("iqhd,ikhd->ihqk", grad_attended, values, preferred_element_type=f32)
    grad_scores = attention * (grad_attention - jnp.sum(attention * grad_attention, axis=-1, keepdims=True))
    grad_scores = grad_scores.astype(bf16)
    grad_query = jnp.einsum("ihqk,ikhd->iqhd", grad_scores, keys, preferred_element_type=f32) * head_scale
    grad_key = jnp.einsum("ihqk,iqhd->ikhd", grad_scores, queries, preferred_element_type=f32) * head_scale
    grad_packed = jnp.stack([grad_query, grad_key, grad_value], axis=2).astype(bf16).reshape(rows, three_width)
    grad_qkv = jnp.dot(hidden_one.T, grad_packed, preferred_element_type=f32)
    grad_hidden_one = jnp.dot(grad_packed, w_qkv.T, preferred_element_type=f32)
    grad_norm_one, grad_gain_one, grad_shift_one = norm_back(grad_hidden_one, normed_one, inverse_one, gain_one)
    grad_tokens = (grad_mixed + grad_norm_one).reshape(images, slots, width)
    return grad_tokens, (grad_gain_one, grad_shift_one, grad_qkv, grad_out, grad_gain_two, grad_shift_two, grad_up, grad_bias)


def contrast(pooled, own_rows, micro_count):
    count = pooled.shape[0]
    images = own_rows // (2 * micro_count)
    inverse = lax.rsqrt(jnp.sum(pooled * pooled, axis=-1, keepdims=True) + unit_epsilon)
    unit = pooled * inverse
    logits = logit_scale * lax.dot_general(unit, unit, (((1,), (1,)), ((), ())), precision=highest, preferred_element_type=f32)
    row = lax.broadcasted_iota(jnp.int32, (count, count), 0)
    col = lax.broadcasted_iota(jnp.int32, (count, count), 1)
    half = own_rows // 2
    row_mod, col_mod = (row // half) % 2, (col // half) % 2
    row_micro, col_micro = (row // images) % micro_count, (col // images) % micro_count
    allowed = (row_mod != col_mod) & (row_micro == col_micro)
    paired = jnp.where(col == row + half * (1 - 2 * row_mod), 1.0, 0.0)
    logits = jnp.where(allowed, logits, masked_score)
    row_max = jnp.max(logits, axis=1, keepdims=True)
    row_lse = row_max + jnp.log(jnp.sum(jnp.exp(logits - row_max), axis=1, keepdims=True))
    col_max = jnp.max(logits, axis=0, keepdims=True)
    col_lse = col_max + jnp.log(jnp.sum(jnp.exp(logits - col_max), axis=0, keepdims=True))
    scale = 1.0 / count
    diagonal = jnp.sum(jnp.where(paired > 0, logits, 0.0), axis=1, keepdims=True)
    loss = scale * jnp.sum(row_lse - diagonal, axis=0, keepdims=True)
    spread = jnp.exp(logits - row_lse) + jnp.exp(logits - col_lse) - 2.0 * paired
    grad_unit = (logit_scale * scale) * jnp.dot(spread, unit, precision=highest, preferred_element_type=f32)
    grad_pooled = inverse * (grad_unit - unit * jnp.sum(unit * grad_unit, axis=-1, keepdims=True))
    return loss, grad_pooled


def meet(peers):
    barrier = pltpu.get_barrier_semaphore()
    for peer in peers:
        pl.semaphore_signal(barrier, inc=1, device_id=(peer,), device_id_type=MESH)
    pl.semaphore_wait(barrier, len(peers))


def gather_kernel(n, micro_count, pooled_ref, sums_ref, loss_ref, grad_ref, got_ref, every, send_sem, recv_sem, sum_send, sum_recv, local_sem):
    me = lax.axis_index("dp")
    rows = pooled_ref.shape[0]
    barrier = pltpu.get_barrier_semaphore()

    def greet(step, carry):
        pl.semaphore_signal(barrier, inc=1, device_id=(lax.rem(me + step, n),), device_id_type=MESH)
        return carry

    lax.fori_loop(1, n, greet, 0)
    pl.semaphore_wait(barrier, n - 1)
    every[me] = pooled_ref[...]
    slot = 0

    def copies(sources, flip, first):
        made = []
        for number, source in enumerate(sources):
            made.append(
                pltpu.make_async_remote_copy(
                    src_ref=every.at[source],
                    dst_ref=every.at[source],
                    send_sem=send_sem.at[first + number],
                    recv_sem=recv_sem.at[first + number],
                    device_id=(me ^ flip,),
                    device_id_type=MESH,
                )
            )
        for copy in made:
            copy.start()
        return made

    def finish(made):
        for copy in made:
            copy.wait()

    held = [me]
    waves = []
    for number, flip in enumerate((8, 16, 24)):
        waves += copies([me], flip, number)
    def sums_out(step, carry):
        peer = lax.rem(me + step, n)
        pltpu.make_async_remote_copy(
            src_ref=sums_ref.at[peer], dst_ref=got_ref.at[me], send_sem=sum_send.at[step], recv_sem=sum_recv.at[step],
            device_id=(peer,), device_id_type=MESH).start()
        return carry

    own = pltpu.make_async_copy(sums_ref.at[me], got_ref.at[me], local_sem)
    own.start()
    finish(waves)
    held = [me, me ^ 8, me ^ 16, me ^ 24]
    wave = copies(held, 4, 3)
    lax.fori_loop(1, n, sums_out, 0)
    finish(wave)
    held = held + [one ^ 4 for one in held]
    finish(copies(held, 2, 7))
    held = held + [one ^ 2 for one in held]
    finish(copies(held, 1, 15))
    loss, grad = contrast(every[...].reshape(n * rows, every.shape[2]), rows, micro_count)
    loss_ref[...] = jnp.broadcast_to(loss, loss_ref.shape)
    grad_ref[...] = grad
    own.wait()

    def sums_in(step, carry):
        peer = lax.rem(me + n - step, n)
        pltpu.make_async_remote_copy(
            src_ref=sums_ref.at[peer], dst_ref=got_ref.at[peer], send_sem=sum_send.at[step], recv_sem=sum_recv.at[step],
            device_id=(peer,), device_id_type=MESH).wait()
        return carry

    lax.fori_loop(1, n, sums_in, 0)


def gather_and_contrast(n, micro_count, pooled, sums):
    rows, width = pooled.shape
    vmem = pl.BlockSpec(memory_space=pltpu.VMEM)
    return pl.pallas_call(
        functools.partial(gather_kernel, n, micro_count),
        out_shape=(
            jax.ShapeDtypeStruct((8, 128), f32),
            jax.ShapeDtypeStruct((n * rows, width), f32),
            jax.ShapeDtypeStruct(sums.shape, f32),
        ),
        in_specs=[vmem, vmem],
        out_specs=(vmem, vmem, vmem),
        scratch_shapes=[
            pltpu.VMEM((n, rows, width), f32),
            pltpu.SemaphoreType.DMA((31,)),
            pltpu.SemaphoreType.DMA((31,)),
            pltpu.SemaphoreType.DMA((n,)),
            pltpu.SemaphoreType.DMA((n,)),
            pltpu.SemaphoreType.DMA,
        ],
        compiler_params=pltpu.CompilerParams(collective_id=0, has_side_effects=True, vmem_limit_bytes=48 << 20),
    )(pooled, sums)


CHUNK = 384


def scatter_kernel(chunks, terms_ref, out_ref, mine, core_got, first_got, second_got, owner_got, sems):
    me = lax.axis_index("dp")
    core, xx, yy, zz = me % 2, (me // 2) % 2, (me // 4) % 2, me // 8
    low_z = zz // 2
    kind = zz % 2
    meet([me ^ 1, me ^ 2, me ^ 4, me ^ 8, me ^ 16, me ^ 24])

    def columns(chunk):
        return pl.ds(pl.multiple_of(chunk * CHUNK, 128), CHUNK)

    def sem(stage, chunk, way):
        return sems.at[stage, chunk, way]

    def take(chunk):
        return pltpu.make_async_copy(terms_ref.at[:, :, :, core, :, columns(chunk)], mine.at[chunk], sem(0, chunk, 0))

    def to_core(chunk):
        return pltpu.make_async_remote_copy(
            src_ref=terms_ref.at[:, :, :, 1 - core, :, columns(chunk)], dst_ref=core_got.at[chunk],
            send_sem=sem(1, chunk, 0), recv_sem=sem(1, chunk, 1), device_id=(me ^ 1,), device_id_type=MESH)

    def first(chunk, along_x):
        src = mine.at[chunk, :, :, 1 - xx] if along_x else mine.at[chunk, :, 1 - yy]
        return pltpu.make_async_remote_copy(
            src_ref=src, dst_ref=first_got.at[chunk],
            send_sem=sem(2, chunk, 0), recv_sem=sem(2, chunk, 1), device_id=(me ^ (2 if along_x else 4),), device_id_type=MESH)

    def second(chunk, along_x):
        src = mine.at[chunk, :, 1 - yy, xx] if along_x else mine.at[chunk, :, yy, 1 - xx]
        return pltpu.make_async_remote_copy(
            src_ref=src, dst_ref=second_got.at[chunk],
            send_sem=sem(3, chunk, 0), recv_sem=sem(3, chunk, 1), device_id=(me ^ (4 if along_x else 2),), device_id_type=MESH)

    def third(chunk, half):
        target = 2 * kind + half
        return target, pltpu.make_async_remote_copy(
            src_ref=mine.at[chunk, half, yy, xx], dst_ref=owner_got.at[chunk, low_z],
            send_sem=sem(4, chunk, half), recv_sem=sem(5, chunk, low_z),
            device_id=(target * 8 + me % 8,), device_id_type=MESH)

    def start_core(chunk, carry):
        take(chunk).start()
        to_core(chunk).start()
        return carry

    lax.fori_loop(0, chunks, start_core, 0)

    def stage(pair, body):
        @pl.when((pair >= 0) & (pair < chunks // 2))
        def _():
            for odd in (0, 1):
                body(2 * pair + odd, odd == 0)

    def run_first(chunk, along_x):
        take(chunk).wait()
        to_core(chunk).wait()
        mine[chunk] = mine[chunk] + core_got[chunk]
        first(chunk, along_x).start()

    def run_second(chunk, along_x):
        first(chunk, along_x).wait()
        if along_x:
            mine[chunk, :, :, xx] = mine[chunk, :, :, xx] + first_got[chunk]
        else:
            mine[chunk, :, yy] = mine[chunk, :, yy] + first_got[chunk]
        second(chunk, along_x).start()

    def run_third(chunk, along_x):
        second(chunk, along_x).wait()
        mine[chunk, :, yy, xx] = mine[chunk, :, yy, xx] + second_got[chunk]
        for half in (0, 1):
            target, copy = third(chunk, half)

            @pl.when(target != zz)
            def _():
                copy.start()

            @pl.when(target == zz)
            def _():
                owner_got[chunk, low_z] = mine[chunk, half, yy, xx]

    def run_last(chunk, along_x):
        for half in (0, 1):
            target, copy = third(chunk, half)

            @pl.when(target != zz)
            def _():
                copy.wait_send()

        for source in (0, 1):
            @pl.when(2 * source + low_z != zz)
            def _():
                pltpu.make_async_remote_copy(
                    src_ref=mine.at[chunk, 0, yy, xx], dst_ref=owner_got.at[chunk, source],
                    send_sem=sem(4, chunk, 0), recv_sem=sem(5, chunk, source),
                    device_id=(me ^ 8,), device_id_type=MESH).wait_recv()

        out_ref[:, columns(chunk)] = owner_got[chunk, 0] + owner_got[chunk, 1]

    def step(pair, carry):
        stage(pair, run_first)
        stage(pair - 1, run_second)
        stage(pair - 2, run_third)
        stage(pair - 3, run_last)
        return carry

    lax.fori_loop(0, chunks // 2 + 3, step, 0)


def scatter_terms(terms):
    rows, columns = terms.shape
    own = rows // 16
    chunks = columns // CHUNK
    return pl.pallas_call(
        functools.partial(scatter_kernel, chunks),
        out_shape=jax.ShapeDtypeStruct((own, columns), f32),
        in_specs=[pl.BlockSpec(memory_space=pl.ANY)],
        out_specs=pl.BlockSpec(memory_space=pltpu.VMEM),
        scratch_shapes=[
            pltpu.VMEM((chunks, 2, 2, 2, own, CHUNK), f32),
            pltpu.VMEM((chunks, 2, 2, 2, own, CHUNK), f32),
            pltpu.VMEM((chunks, 2, 2, own, CHUNK), f32),
            pltpu.VMEM((chunks, 2, own, CHUNK), f32),
            pltpu.VMEM((chunks, 2, own, CHUNK), f32),
            pltpu.SemaphoreType.DMA((6, chunks, 2)),
        ],
        compiler_params=pltpu.CompilerParams(collective_id=1, has_side_effects=True, vmem_limit_bytes=56 << 20),
    )(terms.reshape(2, 2, 2, 2, own, columns))


def params_of(weights, modality):
    return tuple(lax.dynamic_index_in_dim(one, modality, 0, keepdims=False) for one in weights)


def tokens_of(patches, visible, modality):
    micro_count, images, _, patch_count, width = patches.shape
    cells = lax.dynamic_index_in_dim(patches, modality, 2, keepdims=False).reshape(micro_count * images, patch_count, width)
    picked = (visible[:, :, None] == jnp.arange(patch_count)[None, None, :]).astype(bf16)
    return jnp.einsum("isp,ipd->isd", picked, cells, preferred_element_type=f32)


def cells_of(grad_tokens, visible, patch_count):
    picked = (visible[:, None, :] == jnp.arange(patch_count)[None, :, None]).astype(f32)
    return jnp.einsum("ips,isd->ipd", picked, grad_tokens, precision=highest)


def on_device(patches, visible, valid_mask, *weights):
    n = lax.axis_size("dp")
    me = lax.axis_index("dp")
    micro_count, images, _, patch_count, width = patches.shape
    own = micro_count * images
    slots = visible.shape[-1]
    ff = weights[6].shape[2]
    seen = visible.reshape(own, slots)
    mask = valid_mask.reshape(own, slots)
    tuned = n == 32
    kind = (me // 8) % 2 if tuned else 0
    first = params_of(weights, kind)
    other = params_of(weights, 1 - kind)
    tokens_first = tokens_of(patches, seen, kind)
    tokens_other = tokens_of(patches, seen, 1 - kind)
    seen_first, mask_first = seen, mask
    if tuned:
        swap = [(i, i ^ 8) for i in range(n)]
        foreign, seen_there, mask_there = (lax.ppermute(one, "dp", swap) for one in (tokens_other, seen, mask))
        tokens_first = jnp.concatenate([tokens_first, foreign])
        seen_first = jnp.concatenate([seen, seen_there])
        mask_first = jnp.concatenate([mask, mask_there])
    active_first, mixed_first, saved_first = encode_forward(tokens_first, seen_first, mask_first, first)
    active_other, mixed_other, saved_other = encode_forward(tokens_other, seen, mask, other)
    pooled_first = pool(active_first[:own], mixed_first[:own], mask, first[8])
    pooled_other = pool(active_other, mixed_other, mask, other[8])
    counted = jnp.sum(mask.astype(f32), axis=1)[:, None]
    swapped = jnp.asarray(kind == 1)
    pooled = jnp.where(swapped, jnp.concatenate([pooled_other, pooled_first]), jnp.concatenate([pooled_first, pooled_other]))
    share_first, share_other = active_first[:own] / counted, active_other / counted
    shares = jnp.where(swapped, jnp.stack([share_other, share_first]), jnp.stack([share_first, share_other]))
    down_rows = 2 * ff // n
    shares = shares.reshape(2, own, n // 2, down_rows).transpose(0, 2, 1, 3).reshape(n, own * down_rows)
    if tuned:
        padded = jnp.pad(shares, ((0, 0), (0, 1024 - own * down_rows))).reshape(n, 8, 128)
        loss, grad_all, got = gather_and_contrast(n, micro_count, pooled, padded)
        got = got.reshape(n, 1024)[:, : own * down_rows]
    else:
        loss, grad_all = contrast(lax.all_gather(pooled, "dp", axis=0, tiled=True), 2 * own, micro_count)
        got = lax.all_to_all(shares, "dp", 0, 0, tiled=True)
    grad_all = grad_all.reshape(n, 2, own, width)
    holder = me // (n // 2)
    grad_down = jnp.einsum(
        "iw,id->wd", got.reshape(n * own, down_rows),
        lax.dynamic_index_in_dim(grad_all, holder, 1, keepdims=False).reshape(n * own, width), precision=highest)
    mine = lax.dynamic_index_in_dim(grad_all, me, 0, keepdims=False)
    grad_first = lax.dynamic_index_in_dim(mine, kind, 0, keepdims=False)
    grad_other = lax.dynamic_index_in_dim(mine, 1 - kind, 0, keepdims=False)
    if tuned:
        there = lax.dynamic_index_in_dim(grad_all, me ^ 8, 0, keepdims=False)
        grad_first = jnp.concatenate([grad_first, lax.dynamic_index_in_dim(there, kind, 0, keepdims=False)])
    back_first, terms_first = encode_backward(grad_first, saved_first, mask_first, first)
    back_other, terms_other = encode_backward(grad_other, saved_other, mask, other)
    cells_first = cells_of(back_first[:own], seen, patch_count)
    cells_other = cells_of(back_other, seen, patch_count)
    patches_grad = jnp.where(swapped, jnp.stack([cells_other, cells_first], 1), jnp.stack([cells_first, cells_other], 1))
    patches_grad = patches_grad.reshape(micro_count, images, 2, patch_count, width)
    if tuned:
        gain_one, shift_one, qkv, out, gain_two, shift_two, up, bias = terms_first
        small = [one.reshape(width, 1) for one in (gain_one, shift_one, gain_two, shift_two)] + [bias.reshape(width, -1)]
        extra = jnp.concatenate(small, axis=1)
        extra = jnp.pad(extra, ((0, 0), (0, 2 * CHUNK - extra.shape[1])))
        summed = scatter_terms(jnp.concatenate([up, out, qkv, extra], axis=1))
        cuts = [ff, ff + width, ff + 4 * width]
        up, out, qkv, extra = jnp.split(summed, cuts, axis=1)
        shards = (extra[:, 0], extra[:, 1], qkv, out, extra[:, 2], extra[:, 3], up, extra[:, 4 : 4 + ff // width].reshape(-1))
    else:
        joined = jax.tree.map(lambda a, b: jnp.concatenate([a, b]), terms_first, terms_other)
        shards = tuple(lax.psum_scatter(one, "dp", scatter_dimension=0, tiled=True) for one in joined)
    return (loss[0, 0], patches_grad) + shards + (grad_down,)


def solution(mesh):
    in_specs = (P(None, "dp"), P(None, "dp"), P(None, "dp")) + (P(),) * 9
    out_specs = (P(), P(None, "dp")) + (P("dp"),) * 9
    return jax.shard_map(on_device, mesh=mesh, in_specs=in_specs, out_specs=out_specs, check_vma=False)
```

time: 1280 us -> 513 us (0.40)
  waiting for transfers between devices: 558 us -> 0.01 us
  blocking collectives: 203 us -> 0 us
  Pallas kernels: 0 us -> 129 us
  other arithmetic: 183 us -> 83.7 us
  between operations: 21.8 us -> 1.88 us
    reduce_scatter x4 -> x0, waiting for transfers between devices: 436 us -> none  [the longest x1 213 us: on_device(): lax.psum_scatter(joined[6], 'dp', scatter_dimension=0, tiled=True)]
    all_gather x4 -> x0, blocking collectives: 162 us -> none  [the longest x2 84.9 us: on_device(): lax.all_gather(unit_list[0], 'dp', axis=0, tiled=True)]
    pallas_call x0 -> x2, Pallas kernels: none -> 129 us  [the longest x1 106 us: scatter_terms(): pl.pallas_call(functools.partial(scatter_kernel, chunks), out_shape=jax.S...]
    unnamed x6 -> x0, waiting for transfers between devices: 122 us -> none
    scatter-add x4 -> x0, other arithmetic: 96.5 us -> none  [on_device(): cell_grad.at[image_index, visible[micro_index]].add(grad_tokens)]
    unnamed x1 -> x0, blocking collectives: 41.6 us -> none
    another operation x15 -> x2, other arithmetic: 39.6 us -> 4.68 us  [encode_backward(): jnp.stack([grad_query, grad_key, grad_value], axis=2).astype(bf16)]
    unnamed x569 -> x133, local copies, waits for them, and re-layouts: 38.5 us -> 15 us
  transfers between devices with their start and end apart: 5 -> 3, of which waited for: 4 -> 0; matrix products, arithmetic and copies ran while one was open for 17% -> 16% of each run, Pallas kernels for 0% -> 0%
where the time goes in v1:
time: 513 us; the launch traced here: 505 us
  matrix products  186 us (36%)
  Pallas kernels  129 us (25%)
  local copies, waits for them, and re-layouts  99.3 us (19%)
  other arithmetic  83.7 us (16%)
    pallas_call x1, Pallas kernels, scatter_terms(): pl.pallas_call(functools.partial(scatter_kernel, chunks), out_shape=jax.S...  106 us
    dot_general x2, matrix products, encode_forward(): upper = jnp.dot(hidden_two, w_up, preferred_element_type=f32) + b_up  59.4 us
    pallas_call x1, Pallas kernels, gather_and_contrast(): pl.pallas_call(functools.partial(gather_kernel, n, micro_count), out_shap...  22.6 us
    unnamed x133, local copies, waits for them, and re-layouts  15 us
    concatenate x1, other arithmetic, on_device(): summed = scatter_terms(jnp.concatenate([up, out, qkv, extra], axis=1))  14.3 us
    dot_general x2, matrix products, encode_backward(): grad_hidden_two = jnp.dot(grad_upper, w_up.T, preferred_element_type=f32)  13.4 us
    dot_general x2, matrix products, encode_backward(): grad_hidden_one = jnp.dot(grad_packed, w_qkv.T, preferred_element_type=f32)  12.2 us
    select_n x1, other arithmetic, on_device(): jnp.where(swapped, jnp.stack([cells_other, cells_first], 1), jnp.stack([c...  12 us
  transfers between devices with their start and end apart: 3, of which 0 were waited for; matrix products, arithmetic and copies ran while one was open for 16% of the time, Pallas kernels for 0%

profile of v1, /device:TPU:0, one launch (start us, length us, event | category | flops | bytes accessed | tf_op | source)
XLA Modules:
  0.0 505.0 jit_solution(11427982780625751188)
XLA Ops:
  0.7 3.1 collective-permute-start.2
  3.8 10.0 %constant_dynamic-slice_fusion.6 = (bf16[2,2,1,225,768]{4,2,3,1,0:T(2,128)(2,1)}, bf16[2,2,1,225,768]{4,2,3,1,0:T(2,128)(2,1)S(1)}) fusion(bf16[2,2,2,225,768]{4,2,3,1,0:T(2,128)(2,1)} %param.12, s32[]{:T(128)S(6)} %select_n.163, s32[]{:T(128)S(6)} %select_n.159), kind=kLoop, calls=%fused_computation.281 | loop fusion | bytes 5529608 | tf_op jit(solution)/shard_map/jit(dynamic_index_in_dim)/dynamic_slice | solution.py:401
  22.9 3.4 convolution_convert_fusion.1
  26.3 4.4 copy.158
  30.8 5.3 %reshape_reshape.8 = bf16[4,128,3,12,64]{1,0,4,3,2:T(4,128)(2,1)} reshape(bf16[512,2304]{0,1:T(8,128)(2,1)} %copy.158) | data formatting | bytes 4718592 | tf_op jit(solution)/shard_map/reshape;reshape | solution.py:57
  36.1 4.0 fusion.222
  40.3 4.5 fusion.225
  44.9 2.7 fusion.120
  48.2 3.4 multiply_reduce_fusion.13
  55.1 3.2 copy.208
  58.4 20.5 %fusion.19 = (f32[4,3072]{1,0:T(4,128)S(1)}, f32[512,3072]{1,0:T(8,128)}, f32[512,3072]{1,0:T(8,128)}) fusion(f32[4,128]{1,0:T(4,128)S(1)} %convert_element_type.227, f32[3072]{0:T(1024)S(1)} %bitcast.375, bf16[2,768,3072]{2,1,0:T(8,128)(2,1)} %param.21, s32[]{:T(128)S(6)} %select_n.159, f32[512,768]{1,0:T(8,128)S(1)} %copy-done.3, ...), kind=kOutput, calls=%fused_computation.36 | convolution fusion | flops 2526400512 | bytes 18948100 | tf_op jit(solution)/shard_map/dot_general | solution.py:79
  79.0 2.9 fusion.155
  82.0 4.3 fusion.131
  91.7 3.3 add_convert_fusion.1
  96.1 5.4 %convolution_convert_fusion = bf16[1024,2304]{1,0:T(8,128)(2,1)} fusion(bf16[1024,768]{1,0:T(8,128)(2,1)S(1)} %bitcast.362, bf16[2,768,2304]{2,1,0:T(8,128)(2,1)S(1)} %bitcast.390, s32[]{:T(128)S(6)} %select_n.163), kind=kOutput, calls=%fused_computation.65 | convolution fusion | flops 3626237952 | bytes 9830404 | tf_op jit(solution)/shard_map/dot_general | solution.py:67
  101.5 6.6 %copy.165 = bf16[1024,2304]{0,1:T(8,128)(2,1)} copy(bf16[1024,2304]{1,0:T(8,128)(2,1)} %convolution_convert_fusion) | data formatting | bytes 9437184 | tf_op jit(solution)/shard_map/convert_element_type | solution.py:67
  108.1 3.6 copy.213
  114.9 4.5 fusion.223
  119.4 7.0 %fusion.100 = bf16[8,128,12,64]{1,3,2,0:T(8,128)(2,1)} fusion(bf16[8,128,1,12,64]{1,0,4,3,2:T(8,128)(2,1)} %get-tuple-element.51, f32[8,12,128]{2,1,0:T(8,128)S(1)} %get-tuple-element.75, f32[8,12,128,128]{2,3,1,0:T(8,128)} %copy-done.14, f32[8,128,128]{1,2,0:T(8,128)S(1)} %add_sqrt_fusion, f32[12]{0:T(128)S(1)} %exponential_negate_fusion, ...), kind=kOutput, calls=%fused_computation.182 | convolution fusion | flops 213135488 | bytes 10011696 | tf_op jit(solution)/shard_map/ihqk,ikhd->iqhd/dot_general | solution.py:74
  126.4 2.8 copy.170
  129.2 3.3 multiply_reduce_fusion.7
  137.5 39.0 %fusion.3 = (f32[8,3072]{1,0:T(8,128)S(1)}, f32[1024,3072]{1,0:T(8,128)}, f32[1024,3072]{1,0:T(8,128)}) fusion(f32[8,128]{1,0:T(8,128)S(1)} %get-tuple-element.94, f32[3072]{0:T(1024)S(1)} %bitcast.373, bf16[2,768,3072]{2,1,0:T(8,128)(2,1)} %param.21, s32[]{:T(128)S(6)} %select_n.163, f32[1024,768]{1,0:T(8,128)S(1)} %copy-done.1, ...), kind=kOutput, calls=%fused_computation.7 | convolution fusion | flops 5052801024 | bytes 33159172 | tf_op jit(solution)/shard_map/dot_general | solution.py:79
  178.9 22.6 %shard_map.203 = (f32[8,128]{1,0:T(8,128)S(1)}, f32[256,768]{1,0:T(8,128)S(1)}, f32[32,8,128]{2,1,0:T(8,128)S(1)}) custom-call(f32[8,768]{1,0:T(8,128)S(1)} %maximum_select_fusion.2.pooled_ref, f32[32,8,128]{2,1,0:T(8,128)S(1)} %bitcast.334), custom_call_target="tpu_custom_call" | custom-call | tf_op jit(solution)/shard_map/pallas_call | solution.py:241
  203.5 3.7 fusion.46
  207.2 6.4 %fusion.27 = bf16[512,3072]{1,0:T(8,128)(2,1)S(1)} fusion(f32[512,3072]{1,0:T(8,128)} %get-tuple-element.46, f32[512,3072]{1,0:T(8,128)} %get-tuple-element.86, f32[4,3072]{1,0:T(4,128)S(1)} %fusion.46, f32[512]{0:T(512)S(1)} %bitcast.385, f32[3072]{0:T(1024)S(1)} %bitcast.376), kind=kLoop, calls=%fused_computation.45 | loop fusion | flops 25165824 | bytes 15792128 | tf_op jit(solution)/shard_map/convert_element_type | solution.py:107
  213.5 5.2 %fusion.216 = (f32[512]{0:T(512)S(1)}, f32[512]{0:T(512)S(1)}, f32[512,768]{1,0:T(8,128)S(1)}) fusion(f32[512]{0:T(512)S(1)} %add_rsqrt_fusion.2, f32[512,768]{1,0:T(8,128)S(1)} %copy-done.4, f32[512]{0:T(512)S(1)} %broadcast_multiply_fusion.11, f32[768]{0:T(1024)S(1)} %get-tuple-element.33, bf16[512,3072]{1,0:T(8,128)(2,1)S(1)} %fusion.27, ...), kind=kOutput, calls=%fused_computation.350 | convolution fusion | flops 2418277376 | bytes 11021316 | tf_op jit(solution)/shard_map/dot_general | solution.py:110
  224.6 4.4 fusion.121
  237.4 9.3 %convert_reduce_fusion = (f32[3072]{0:T(1024)S(1)}, bf16[1024,3072]{1,0:T(8,128)(2,1)S(1)}) fusion(f32[1024,3072]{1,0:T(8,128)S(1)} %bitcast.338, f32[8,3072]{1,0:T(8,128)S(1)} %fusion.38, f32[1024]{0:T(1024)S(1)} %fusion.188, f32[1024,3072]{1,0:T(8,128)} %get-tuple-element.79, f32[3072]{0:T(1024)S(1)} %bitcast.374), kind=kLoop, calls=%fused_computation.18 | loop fusion | flops 56620032 | bytes 31584256 | tf_op jit(solution)/shard_map/reduce_sum | solution.py:108
  246.7 8.2 %multiply_reduce_fusion.1 = (f32[768]{0:T(1024)S(1)}, f32[1024]{0:T(1024)S(1)}, f32[1024]{0:T(1024)S(1)}, f32[768]{0:T(1024)S(1)}, f32[1024,768]{1,0:T(8,128)S(1)}) fusion(f32[1024,768]{1,0:T(8,128)S(1)} %copy-done.2, f32[1024]{0:T(1024)S(1)} %add_rsqrt_fusion, f32[1024]{0:T(1024)S(1)} %broadcast_multiply_fusion.5, f32[768]{0:T(1024)S(1)} %get-tuple-element.34, ...), kind=kOutput, calls=%fused_computation.111 | convolution fusion | flops 4838912000 | bytes 17327108 | tf_op jit(solution)/shard_map/dot_general | solution.py:110
  254.9 8.5 %fusion.212 = f32[768,3072]{1,0:T(8,128)} fusion(bf16[1024,3072]{1,0:T(8,128)(2,1)S(1)} %get-tuple-element.42, f32[1024,768]{1,0:T(8,128)S(1)} %copy-done.2, f32[768]{0:T(1024)S(1)} %get-tuple-element.97, f32[768]{0:T(1024)S(1)} %get-tuple-element.34, f32[1024]{0:T(1024)S(1)} %add_rsqrt_fusion, f32[1024]{0:T(1024)S(1)} %broadcast_multiply_fusion.5), kind=kOutput, calls=%fused_computation.346 | convolution fusion | flops 4835770368 | bytes 18888704 | tf_op jit(solution)/shard_map/dot_general | solution.py:109
  264.9 2.8 fusion.84
  267.7 2.7 convolution_convert_fusion.3
  270.3 2.8 copy.179
  273.1 3.1 copy.217
  276.2 7.1 %fusion.103 = bf16[8,128,1,12,64]{1,4,3,0,2:T(8,128)(2,1)} fusion(bf16[8,128,12,64]{1,0,3,2:T(8,128)(2,1)} %bitcast.360, f32[8,12,128]{2,1,0:T(8,128)S(1)} %get-tuple-element.75, f32[8,12,128,128]{2,3,1,0:T(8,128)} %copy-done.14, f32[8,128,128]{1,2,0:T(8,128)} %copy-done.30, f32[12]{0:T(128)S(1)} %exponential_negate_fusion, pred[8,128]{1,0:T(8,128)(4,1)S(1)} %fusion.191), kind=kOutput, calls=%fused_computation.183 | convolution fusion | flops 213135488 | bytes 10011696 | tf_op jit(solution)/shard_map/ihqk,iqhd->ikhd/dot_general | solution.py:118
  283.3 8.0 %multiply_reduce_fusion = (f32[8,12,128]{2,1,0:T(8,128)S(1)}, f32[8,12,128,128]{2,3,1,0:T(8,128)}) fusion(f32[8,12,128,128]{2,3,1,0:T(8,128)} %get-tuple-element.76, f32[8,12,128]{2,1,0:T(8,128)S(1)} %get-tuple-element.75, bf16[8,128,1,12,64]{1,0,4,3,2:T(8,128)(2,1)} %get-tuple-element.51, bf16[8,128,12,64]{1,0,3,2:T(8,128)(2,1)} %bitcast.361), kind=kOutput, calls=%fused_computation.48 | convolution fusion | flops 206032896 | bytes 15826944 | tf_op jit(solution)/shard_map/iqhd,ikhd->ihqk/dot_general | solution.py:119
  291.3 5.0 multiply_convert_fusion.1
  296.3 3.5 fusion.99
  304.9 3.1 pad_maximum_fusion
  308.0 9.3 %copy.185 = bf16[8,128,3,12,64]{1,0,4,3,2:T(8,128)(2,1)S(1)} copy(bf16[8,128,3,12,64]{1,4,3,0,2:T(8,128)(2,1)S(1)} %pad_maximum_fusion) | data formatting | bytes 9437184 | tf_op jit(solution)/shard_map/stack | solution.py:124
  317.4 6.0 %fusion.34 = f32[768,2304]{1,0:T(8,128)} fusion(bf16[1024,768]{1,0:T(8,128)(2,1)S(1)} %bitcast.363, bf16[288,8,8,128]{3,2,1,0:T(8,128)(2,1)S(1)} %bitcast.356), kind=kOutput, calls=%fused_computation.67 | convolution fusion | flops 3623878656 | bytes 13369344 | tf_op jit(solution)/shard_map/dot_general | solution.py:125
  323.4 7.1 %fusion.214 = (f32[768]{0:T(1024)S(1)}, f32[768]{0:T(1024)S(1)}, f32[1024]{0:T(1024)S(1)}, f32[1024]{0:T(1024)S(1)}, f32[1024,768]{1,0:T(8,128)}, /*index=5*/f32[1024,768]{1,0:T(8,128)}) fusion(f32[768]{0:T(1024)S(1)} %copy-done.38, f32[1024]{0:T(1024)S(1)} %get-tuple-element.65, f32[1024]{0:T(1024)S(1)} %copy-done.45, f32[8,128,768]{2,1,0:T(8,128)S(1)} %copy-done.11, ...), kind=kOutput, calls=%fused_computation.348 | convolution fusion | flops 3630952960 | bytes 17721348 | tf_op jit(solution)/shard_map/dot_general | solution.py:126
  334.9 14.3 %select_maximum_fusion = f32[768,6912]{1,0:T(8,128)} fusion(f32[768,8]{1,0:T(8,128)} %concatenate.87, f32[768,2304]{1,0:T(8,128)} %fusion.34, f32[768,768]{1,0:T(8,128)} %fusion.84, f32[768,3072]{1,0:T(8,128)} %fusion.212), kind=kLoop, calls=%fused_computation.2 | loop fusion | flops 26542080 | bytes 40132608 | tf_op jit(solution)/shard_map/concatenate | solution.py:473
  349.2 106.1 %shard_map.204 = f32[48,6912]{1,0:T(8,128)} custom-call(f32[2,2,2,2,48,6912]{5,4,3,2,1,0:T(8,128)} %bitcast.336), custom_call_target="tpu_custom_call" | custom-call | tf_op jit(solution)/shard_map/pallas_call | solution.py:378
  471.3 5.0 fusion.215
  479.7 4.4 copy.186
  486.2 4.4 copy.187
  492.7 12.0 %maximum_select_fusion = f32[2,2,2,225,768]{4,2,3,1,0:T(2,128)} fusion(f32[2,2,1,225,768]{4,2,3,1,0:T(1,128)} %copy.187, f32[2,2,1,225,768]{4,2,3,1,0:T(1,128)} %copy.186, pred[]{:T(512)S(6)} %eq.22), kind=kLoop, calls=%fused_computation.66 | loop fusion | flops 4147200 | bytes 11059201 | tf_op jit(solution)/shard_map/jit(_where)/select_n | solution.py:466
  (237 shorter events, 81.0 us)
Async XLA Ops:
  0.6 47.5 %copy-start = (bf16[2,768,768]{2,1,0:T(8,128)(2,1)S(1)}, bf16[2,768,768]{2,1,0:T(8,128)(2,1)}, u32[]{:S(2)}) copy-start(bf16[2,768,768]{2,1,0:T(8,128)(2,1)} %param.18) | copy-start | bytes 7077892
  0.7 85.7 %collective-permute-start.2 = (s32[4,128]{1,0:T(4,128)}, s32[4,128]{1,0:T(4,128)S(1)}, u32[]{:S(2)}, u32[]{:S(2)}) collective-permute-start(s32[4,128]{1,0:T(4,128)} %bitcast.377), channel_id=1, source_target_pairs={{0,8},{1,9},{2,10},{3,11},{4,12},{5,13},{6,14},{7,15},{8,0},{9,1},... | collective-permute-start | bytes 6152 | tf_op jit(solution)/shard_map/ppermute | solution.py:429
  3.7 82.5 %collective-permute-start.1 = (s32[4,128]{1,0:T(4,128)}, s32[4,128]{1,0:T(4,128)S(1)}, u32[]{:S(2)}, u32[]{:S(2)}) collective-permute-start(s32[4,128]{1,0:T(4,128)} %bitcast.366), channel_id=1, source_target_pairs={{0,8},{1,9},{2,10},{3,11},{4,12},{5,13},{6,14},{7,15},{8,0},{9,1},... | collective-permute-start | bytes 6152 | tf_op jit(solution)/shard_map/ppermute | solution.py:429
  3.8 19.0 %slice-start.11 = ((s8[7077888]{0:T(1024)(128)(4,1)}), s8[4194304]{0:T(1024)(128)(4,1)S(1)}, s32[]{:S(2)}) async-start(s8[7077888]{0:T(1024)(128)(4,1)} %bitcast.387), calls=%async_computation.11 | async-start | bytes 8388608
  13.8 4.2 copy-start.31
  13.8 4.3 copy-start.34
  13.8 9.0 %slice-start.12 = ((s8[7077888]{0:T(1024)(128)(4,1)}), s8[2883584]{0:T(1024)(128)(4,1)S(1)}, s32[]{:S(2)}) async-start(s8[7077888]{0:T(1024)(128)(4,1)} %bitcast.387), calls=%async_computation.12 | async-start | bytes 5767168
  14.1 7.0 %copy-start.41 = (f32[2,768]{1,0:T(2,128)S(1)}, f32[2,768]{1,0:T(2,128)}, u32[]{:S(2)}) copy-start(f32[2,768]{1,0:T(2,128)} %param.15) | copy-start | bytes 18436
  14.1 7.0 %copy-start.42 = (f32[2,768]{1,0:T(2,128)S(1)}, f32[2,768]{1,0:T(2,128)}, u32[]{:S(2)}) copy-start(f32[2,768]{1,0:T(2,128)} %param.16) | copy-start | bytes 18436
  16.1 70.7 %collective-permute-start = (f32[4,128,768]{2,1,0:T(8,128)}, f32[4,128,768]{2,1,0:T(8,128)}, u32[]{:S(2)}, u32[]{:S(2)}) collective-permute-start(f32[4,128,768]{2,1,0:T(8,128)} %get-tuple-element.81), channel_id=1, source_target_pairs={{0,8},{1,9},{2,10},{3,11},{4,12},{5,13},{6,14},{7,15},{8,0},{9,1},... | collective-permute-start | bytes 4718600 | tf_op jit(solution)/shard_map/ppermute | solution.py:429
  21.1 5.2 %copy-start.35 = (f32[768]{0:T(1024)}, f32[768]{0:T(1024)S(1)}, u32[]{:S(2)}) copy-start(f32[768]{0:T(1024)S(1)} %get-tuple-element.37) | copy-start | bytes 9220
  21.1 70.5 %copy-start.37 = (f32[768]{0:T(1024)}, f32[768]{0:T(1024)S(1)}, u32[]{:S(2)}) copy-start(f32[768]{0:T(1024)S(1)} %get-tuple-element.38) | copy-start | bytes 9220
  40.1 4.8 copy-start.19
  53.2 5.1 %copy-start.43 = (f32[2,768]{1,0:T(2,128)S(1)}, f32[2,768]{1,0:T(2,128)}, u32[]{:S(2)}) copy-start(f32[2,768]{1,0:T(2,128)} %param.19) | copy-start | bytes 18436
  53.2 5.1 %copy-start.44 = (f32[2,768]{1,0:T(2,128)S(1)}, f32[2,768]{1,0:T(2,128)}, u32[]{:S(2)}) copy-start(f32[2,768]{1,0:T(2,128)} %param.20) | copy-start | bytes 18436
  86.2 3.5 copy-start.5
  86.8 32.6 %copy-start.30 = (f32[8,128,128]{1,2,0:T(8,128)}, f32[8,128,128]{1,2,0:T(8,128)S(1)}, u32[]{:S(2)}) copy-start(f32[8,128,128]{1,2,0:T(8,128)S(1)} %add_sqrt_fusion) | copy-start | bytes 1572868
  86.8 9.3 %slice-start.13 = ((s8[7077888]{0:T(1024)(128)(4,1)}), s8[4194304]{0:T(1024)(128)(4,1)S(1)}, s32[]{:S(2)}) async-start(s8[7077888]{0:T(1024)(128)(4,1)} %bitcast.389), calls=%async_computation.13 | async-start | bytes 8388608
  91.6 4.4 slice-start.14
  114.9 4.5 copy-start.14
  134.6 41.9 %slice-start.3 = ((s8[9437184]{0:T(1024)(128)(4,1)}), s8[4194304]{0:T(1024)(128)(4,1)S(1)}, s32[]{:S(2)}) async-start(s8[9437184]{0:T(1024)(128)(4,1)} %bitcast.339), calls=%async_computation.3 | async-start | bytes 8388608
  137.5 39.1 %slice-start.4 = ((s8[9437184]{0:T(1024)(128)(4,1)}), s8[4194304]{0:T(1024)(128)(4,1)S(1)}, s32[]{:S(2)}) async-start(s8[9437184]{0:T(1024)(128)(4,1)} %bitcast.339), calls=%async_computation.4 | async-start | bytes 8388608
  137.5 39.1 %slice-start.5 = ((s8[9437184]{0:T(1024)(128)(4,1)}), s8[1048576]{0:T(1024)(128)(4,1)S(1)}, s32[]{:S(2)}) async-start(s8[9437184]{0:T(1024)(128)(4,1)} %bitcast.339), calls=%async_computation.5 | async-start | bytes 2097152
  207.2 6.4 %copy-start.4 = (f32[512,768]{1,0:T(8,128)S(1)}, f32[512,768]{1,0:T(8,128)}, u32[]{:S(2)}) copy-start(f32[512,768]{1,0:T(8,128)} %get-tuple-element.85) | copy-start | bytes 4718596
  224.6 4.4 copy-start.22
  224.6 4.4 copy-start.26
  224.6 4.4 copy-start.27
  229.0 6.8 %slice-start.6 = ((s8[9437184]{0:T(1024)(128)(4,1)}), s8[4194304]{0:T(1024)(128)(4,1)S(1)}, s32[]{:S(2)}) async-start(s8[9437184]{0:T(1024)(128)(4,1)} %bitcast.341), calls=%async_computation.6 | async-start | bytes 8388608
  229.0 6.8 %slice-start.7 = ((s8[9437184]{0:T(1024)(128)(4,1)}), s8[4194304]{0:T(1024)(128)(4,1)S(1)}, s32[]{:S(2)}) async-start(s8[9437184]{0:T(1024)(128)(4,1)} %bitcast.341), calls=%async_computation.7 | async-start | bytes 8388608
  229.0 8.3 %slice-start = ((s8[12582912]{0:T(1024)(128)(4,1)}), s8[4194304]{0:T(1024)(128)(4,1)S(1)}, s32[]{:S(2)}) async-start(s8[12582912]{0:T(1024)(128)(4,1)} %bitcast.337), calls=%async_computation | async-start | bytes 8388608
  229.0 8.3 %slice-start.1 = ((s8[12582912]{0:T(1024)(128)(4,1)}), s8[4194304]{0:T(1024)(128)(4,1)S(1)}, s32[]{:S(2)}) async-start(s8[12582912]{0:T(1024)(128)(4,1)} %bitcast.337), calls=%async_computation.1 | async-start | bytes 8388608
  229.9 6.1 %slice-start.8 = ((s8[9437184]{0:T(1024)(128)(4,1)}), s8[1048576]{0:T(1024)(128)(4,1)S(1)}, s32[]{:S(2)}) async-start(s8[9437184]{0:T(1024)(128)(4,1)} %bitcast.341), calls=%async_computation.8 | async-start | bytes 2097152
  231.5 5.9 %slice-start.2 = ((s8[12582912]{0:T(1024)(128)(4,1)}), s8[4194304]{0:T(1024)(128)(4,1)S(1)}, s32[]{:S(2)}) async-start(s8[12582912]{0:T(1024)(128)(4,1)} %bitcast.337), calls=%async_computation.2 | async-start | bytes 8388608
  237.4 9.3 %copy-start.2 = (f32[1024,768]{1,0:T(8,128)S(1)}, f32[1024,768]{1,0:T(8,128)}, u32[]{:S(2)}) copy-start(f32[1024,768]{1,0:T(8,128)} %get-tuple-element.78) | copy-start | bytes 9437188
  283.3 8.0 %slice-start.9 = ((s8[6291456]{0:T(1024)(128)(4,1)}), s8[4194304]{0:T(1024)(128)(4,1)S(1)}, s32[]{:S(2)}) async-start(s8[6291456]{0:T(1024)(128)(4,1)} %bitcast.350), calls=%async_computation.9 | async-start | bytes 8388608
  283.3 8.0 %slice-start.10 = ((s8[6291456]{0:T(1024)(128)(4,1)}), s8[2097152]{0:T(1024)(128)(4,1)S(1)}, s32[]{:S(2)}) async-start(s8[6291456]{0:T(1024)(128)(4,1)} %bitcast.350), calls=%async_computation.10 | async-start | bytes 4194304
  291.3 5.0 copy-start.9
  307.9 9.4 %copy-start.25 = (bf16[8,128,768]{2,1,0:T(8,128)(2,1)S(1)}, bf16[8,128,768]{2,1,0:T(8,128)(2,1)}, u32[]{:S(2)}) copy-start(bf16[8,128,768]{2,1,0:T(8,128)(2,1)} %copy-done.24) | copy-start | bytes 4718596
  308.0 15.4 %slice-start.15 = ((s8[7077888]{0:T(1024)(128)(4,1)}), s8[4194304]{0:T(1024)(128)(4,1)S(1)}, s32[]{:S(2)}) async-start(s8[7077888]{0:T(1024)(128)(4,1)} %bitcast.391), calls=%async_computation.15 | async-start | bytes 8388608
  317.3 6.0 %copy-start.11 = (f32[8,128,768]{2,1,0:T(8,128)S(1)}, f32[8,128,768]{2,1,0:T(8,128)}, u32[]{:S(2)}) copy-start(f32[8,128,768]{2,1,0:T(8,128)} %get-tuple-element.53) | copy-start | bytes 9437188
  317.3 6.0 %copy-start.38 = (f32[768]{0:T(1024)S(1)}, f32[768]{0:T(1024)}, u32[]{:S(2)}) copy-start(f32[768]{0:T(1024)} %copy-done.37) | copy-start | bytes 9220
  317.3 6.0 %copy-start.45 = (f32[1024]{0:T(1024)S(1)}, f32[1024]{0:T(1024)}, u32[]{:S(2)}) copy-start(f32[1024]{0:T(1024)} %get-tuple-element.63) | copy-start | bytes 12292
  317.3 6.0 %slice-start.16 = ((s8[7077888]{0:T(1024)(128)(4,1)}), s8[2883584]{0:T(1024)(128)(4,1)S(1)}, s32[]{:S(2)}) async-start(s8[7077888]{0:T(1024)(128)(4,1)} %bitcast.391), calls=%async_computation.16 | async-start | bytes 5767168
  471.3 5.1 %copy-start.16 = (f32[512,768]{1,0:T(8,128)S(1)}, f32[512,768]{1,0:T(8,128)}, u32[]{:S(2)}) copy-start(f32[512,768]{1,0:T(8,128)} %copy-done.15) | copy-start | bytes 4718596
  478.3 5.8 %copy-start.28 = (f32[1024,768]{1,0:T(8,128)S(1)}, f32[1024,768]{1,0:T(8,128)}, u32[]{:S(2)}) copy-start(f32[1024,768]{1,0:T(8,128)} %get-tuple-element.43) | copy-start | bytes 9437188
  478.3 5.8 %copy-start.29 = (f32[1024,768]{1,0:T(8,128)S(1)}, f32[1024,768]{1,0:T(8,128)}, u32[]{:S(2)}) copy-start(f32[1024,768]{1,0:T(8,128)} %get-tuple-element.44) | copy-start | bytes 9437188
  479.7 4.4 copy-start.13
  486.1 5.1 %copy-start.23 = (f32[128,768]{1,0:T(8,128)S(1)}, f32[128,768]{1,0:T(8,128)}, u32[]{:S(2)}) copy-start(f32[128,768]{1,0:T(8,128)} %reshape.856) | copy-start | bytes 1179652
  (18 other events, 38.8 us)
